TPU v7x, 512 devices: a whole 4x4x16 slice. The times are simulated.
512 devices in a mesh: subj: 32 (over z, core), var: 16 (over x, y).
Axes of the slice: x: 4, y: 4, z: 16, core: 2. Of those that a mesh axis runs over, the one named last changes fastest.
Arguments:
- traits: bfloat16 [65536, 256], P('subj', 'var'), may hold values from -6 to 6
- kin_tiles: bfloat16 [384, 256, 256], P('subj'), may hold values from -0.25 to 0.25
- kin_index: int32 [384, 2], P('subj'), may hold values from 0 to 255, as said below
- dosages: bfloat16 [65536, 12288], P('subj', 'var'), may hold values from 0 to 255, as said below
Outputs:
- scores: float32 [12288, 256], P(('var', 'subj'))
Inputs may be any that keep to these rules, and one draw needn't show every extreme that they name: `kin_index`: rows t * 12 to (t + 1) * 12 - 1 hold tiles whose row block lies in t * 8 to (t + 1) * 8 - 1; every row block has its diagonal tile; counts per row block are uneven; a pair may repeat. `dosages`: whole numbers.
All inputs are finite; a program needn't handle non-finite values.
Results may differ from a plain program's by a relative error of at most 0.009.
Values may be sent and summed in bfloat16 or wider, within the bound.
No kernel may reach another device: no remote copies, remote signals or barrier semaphores. Data moves between devices by JAX's collectives and lax.ppermute only.
A program may use at most 64 MiB of HBM per device.

v0:
```python
import jax
import jax.numpy as jnp
from jax import lax
from jax.sharding import PartitionSpec as P


def sent_to_all(x, axis):
    copies = jnp.broadcast_to(x, (lax.axis_size(axis), *x.shape))
    return lax.all_to_all(copies, axis, split_axis=0, concat_axis=0, tiled=True)


def laid_out(blocks, dim):
    blocks = jnp.moveaxis(blocks, 0, dim)
    dims = blocks.shape
    return blocks.reshape(*dims[:dim], dims[dim] * dims[dim + 1], *dims[dim + 2 :])


def gathered_copies(x, axis, dim):
    blocks = sent_to_all(x, axis)
    return laid_out(blocks, dim)


def cut_along(x, dim, devices):
    dims = x.shape
    blocks = x.reshape(*dims[:dim], devices, dims[dim] // devices, *dims[dim + 1 :])
    return jnp.moveaxis(blocks, dim, 0)


def sum_at_owner(x, axis, dim):
    blocks = cut_along(x, dim, lax.axis_size(axis))
    arrived = lax.all_to_all(blocks, axis, split_axis=0, concat_axis=0, tiled=True)
    return arrived.sum(axis=0)


def kinship_apply(field, kin_tiles, kin_index):
    rows_here = field.shape[0]
    block = kin_tiles.shape[1]
    width = field.shape[1]
    blocks_dev = rows_here // block
    gathered = lax.all_gather(field, "subj", axis=0, tiled=True)
    slabs = gathered.reshape(-1, block, width)[kin_index[:, 1]]
    prods = jnp.einsum("tij,tjk->tik", kin_tiles, slabs, preferred_element_type=jnp.float32)
    row_local = kin_index[:, 0] - lax.axis_index("subj") * blocks_dev
    onehot = (row_local[None, :] == jnp.arange(blocks_dev, dtype=jnp.int32)[:, None]).astype(
        jnp.float32
    )
    summed = jnp.einsum("bt,tik->bik", onehot, prods)
    return summed.reshape(rows_here, width)


def on_device(traits, kin_tiles, kin_index, dosages):
    first = kinship_apply(traits, kin_tiles, kin_index)
    first_sent = first.astype(jnp.bfloat16)
    second = kinship_apply(first_sent, kin_tiles, kin_index)
    base = traits.astype(jnp.float32)
    whitened = (0.6 * base + 0.5 * first + 0.3 * (2.0 * second - base)).astype(jnp.bfloat16)
    subjects = traits.shape[0] * lax.axis_size("subj")
    scale = 1.0 / (127.5 * jnp.sqrt(jnp.float32(subjects)))
    contract = (((0,), (0,)), ((), ()))
    wide = gathered_copies(whitened, "var", 1)
    partial_scores = lax.dot_general(dosages, wide, contract, preferred_element_type=jnp.float32)
    scores = sum_at_owner(partial_scores, "subj", 0)
    return scores * scale


def solution(mesh):
    in_specs = (P("subj", "var"), P("subj", None, None), P("subj", None), P("subj", "var"))
    out_specs = P(("var", "subj"), None)
    return jax.shard_map(
        on_device, mesh=mesh, in_specs=in_specs, out_specs=out_specs, check_vma=False
    )
```

profile of v0, /device:TPU:1, one launch (start us, length us, event | category | flops | bytes accessed | tf_op | source)
XLA Modules:
  0.0 261.5 jit_solution(4800661068077211716)
XLA Ops:
  6.5 0.0 copy-start
  6.5 0.0 all-gather.3.cloned.1.call-start
  6.5 0.7 all-gather.3.cloned.1.call-update
  7.3 0.0 all-gather.5.cloned.1.call-start
  7.3 0.9 subtract_bitcast_fusion
  8.2 78.9 %all-gather.3.cloned.1.call-done = bf16[65536,16]{0,1:T(8,128)(2,1)} async-done(((bf16[2048,16]{0,1:T(8,128)(2,1)}), bf16[65536,16]{0,1:T(8,128)(2,1)}) %all-gather.3.cloned.1.call-update) | async-done | bytes 2097168 | tf_op jit(solution)/shard_map/all_gather | solution.py:40
  87.1 3.1 %copy.26 = bf16[2,256,8,256]{3,2,0,1:T(8,128)(2,1)} copy(bf16[2,256,8,256]{3,2,1,0:T(8,128)(2,1)} %bitcast.49) | data formatting | bytes 4194304 | tf_op jit(solution)/shard_map/reshape | solution.py:41
  90.1 2.1 gather_fusion
  92.3 1.9 convolution_bitcast_fusion.2
  94.2 0.2 fusion.13
  94.4 0.6 copy.15
  95.0 0.0 all-gather.5.cloned.1.call-update
  95.1 68.9 %all-gather.5.cloned.1.call-done = bf16[65536,16]{0,1:T(8,128)(2,1)} async-done(((bf16[2048,16]{0,1:T(8,128)(2,1)}), bf16[65536,16]{0,1:T(8,128)(2,1)}) %all-gather.5.cloned.1.call-update) | async-done | bytes 2097168 | tf_op jit(solution)/shard_map/all_gather | solution.py:40
  164.0 3.1 %copy.25 = bf16[2,256,8,256]{3,2,0,1:T(8,128)(2,1)} copy(bf16[2,256,8,256]{3,2,1,0:T(8,128)(2,1)} %bitcast.50) | data formatting | bytes 4194304 | tf_op jit(solution)/shard_map/reshape | solution.py:41
  167.1 0.0 copy-start.1
  167.1 2.2 gather_fusion.1
  169.2 1.9 convolution_bitcast_fusion.1
  171.2 0.2 convolution_multiply_fusion
  171.4 0.0 copy-done.1
  171.4 0.1 broadcast_in_dim.2
  171.6 22.3 %all_to_all.10 = bf16[16,2048,16]{1,2,0:T(8,128)(2,1)S(1)} all-to-all(bf16[16,2048,16]{1,2,0:T(8,128)(2,1)S(1)} %broadcast_in_dim.2), channel_id=1, replica_groups=mesh['subj'=32,'var'=16] {'var'}, dimensions={0} | all-to-all | bytes 2097152 | tf_op jit(solution)/shard_map/all_to_all | solution.py:9
  193.8 0.0 copy-done
  193.8 1.9 convolution_bitcast_fusion
  195.7 2.3 copy.11
  198.0 54.9 %all_to_all.11 = f32[32,24,256]{2,1,0:T(8,128)} all-to-all(f32[32,24,256]{2,1,0:T(8,128)} %bitcast.48), channel_id=1, replica_groups=mesh['subj'=32,'var'=16] {'subj'}, dimensions={0} | all-to-all | bytes 1572864 | tf_op jit(solution)/shard_map/all_to_all | solution.py:31
  252.8 1.2 reduce_sum.9
  254.0 0.6 broadcast_multiply_fusion.1
  (4 shorter events, 0.1 us)
Async XLA Ops:
  6.5 187.3 %copy-start = (bf16[2048,768]{1,0:T(8,128)(2,1)S(1)}, bf16[2048,768]{1,0:T(8,128)(2,1)}, u32[]{:S(2)}) copy-start(bf16[2048,768]{1,0:T(8,128)(2,1)} %param.7) | copy-start | bytes 9437188
  6.5 80.5 %all-gather.3.cloned.1.call-start = ((), (), s32[]{:S(2)}) async-start(), calls=%async_computation.2 | async-start | bytes 2162688 | tf_op jit(solution)/shard_map/all_gather | solution.py:40
  7.3 156.7 %all-gather.5.cloned.1.call-start = ((), (), s32[]{:S(2)}) async-start(), calls=%async_computation.3 | async-start | bytes 2162688 | tf_op jit(solution)/shard_map/all_gather | solution.py:40
  167.1 4.3 %copy-start.1 = (bf16[2048,16]{0,1:T(8,128)(2,1)S(1)}, bf16[2048,16]{0,1:T(8,128)(2,1)}, u32[]{:S(2)}) copy-start(bf16[2048,16]{0,1:T(8,128)(2,1)} %param.4) | copy-start | bytes 196612
Sparse Core Ops, SparseCore 0:
  9.5 77.5 all-gather.2
  95.2 68.7 all-gather.4
where the time goes:
time: 262 us; the launch traced here: 261 us
  waiting for transfers between devices  149 us (57%)
  blocking collectives  77.1 us (29%)
  local copies, waits for them, and re-layouts  13.6 us (5%)
  between operations  13.5 us (5%)
  matrix products  6.06 us (2%)
  other arithmetic  2.72 us (1%)
    all_gather x2, waiting for transfers between devices, kinship_apply(): gathered = lax.all_gather(field, 'subj', axis=0, tiled=True)  148 us
    all_to_all x1, blocking collectives, sum_at_owner(): lax.all_to_all(blocks, axis, split_axis=0, concat_axis=0, tiled=True)  54.9 us
    all_to_all x1, blocking collectives, sent_to_all(): return lax.all_to_all(copies, axis, split_axis=0, concat_axis=0, tiled=True)  22.3 us
    reshape x2, local copies, waits for them, and re-layouts, kinship_apply(): slabs = gathered.reshape(-1, block, width)[kin_index[:, 1]]  6.13 us
  transfers between devices with their start and end apart: 2, of which 2 were waited for; matrix products, arithmetic and copies ran while one was open for 0% of the time, Pallas kernels for 0%

commit v1 on v0

--- a/solution.py
+++ b/solution.py
@@ -37,7 +37,9 @@
     block = kin_tiles.shape[1]
     width = field.shape[1]
     blocks_dev = rows_here // block
-    gathered = lax.all_gather(field, "subj", axis=0, tiled=True)
+    gathered = jnp.concatenate(
+        lax.all_to_all(jnp.stack([field] * lax.axis_size("subj")), "subj", 0, 0), axis=0
+    )
     slabs = gathered.reshape(-1, block, width)[kin_index[:, 1]]
     prods = jnp.einsum("tij,tjk->tik", kin_tiles, slabs, preferred_element_type=jnp.float32)
     row_local = kin_index[:, 0] - lax.axis_index("subj") * blocks_dev

time: 262 us -> 338 us (1.29)
  waiting for transfers between devices: 149 us -> 198 us
  starting transfers between devices: 0.04 us -> 22.2 us
  local copies, waits for them, and re-layouts: 13.6 us -> 35.6 us
  between operations: 13.5 us -> 0.11 us
  blocking collectives: 77.1 us -> 73.5 us
    all_to_all x0 -> x2, waiting for transfers between devices: none -> 198 us  [kinship_apply(): lax.all_to_all(jnp.stack([field] * lax.axis_size('subj')), 'subj', 0, 0)]
    all_gather x2 -> x0, waiting for transfers between devices: 148 us -> none  [kinship_apply(): gathered = lax.all_gather(field, 'subj', axis=0, tiled=True)]
    all_to_all x0 -> x2, starting transfers between devices: none -> 22.2 us  [kinship_apply(): lax.all_to_all(jnp.stack([field] * lax.axis_size('subj')), 'subj', 0, 0)]
    another operation x0 -> x6, local copies, waits for them, and re-layouts: none -> 20.7 us  [the longest x4 16.5 us: kinship_apply(): slabs = gathered.reshape(-1, block, width)[kin_index[:, 1]]]
    all_to_all x0 -> x2, local copies, waits for them, and re-layouts: none -> 8.11 us  [kinship_apply(): lax.all_to_all(jnp.stack([field] * lax.axis_size('subj')), 'subj', 0, 0)]
    reshape x2 -> x0, local copies, waits for them, and re-layouts: 6.13 us -> none  [kinship_apply(): slabs = gathered.reshape(-1, block, width)[kin_index[:, 1]]]
where the time goes in v1:
time: 338 us; the launch traced here: 337 us
  waiting for transfers between devices  198 us (59%)
  blocking collectives  73.5 us (22%)
  local copies, waits for them, and re-layouts  35.6 us (11%)
  starting transfers between devices  22.2 us (7%)
  matrix products  6.04 us (2%)
    all_to_all x2, waiting for transfers between devices, kinship_apply(): lax.all_to_all(jnp.stack([field] * lax.axis_size('subj')), 'subj', 0, 0)  198 us
    all_to_all x1, blocking collectives, sum_at_owner(): lax.all_to_all(blocks, axis, split_axis=0, concat_axis=0, tiled=True)  53.6 us
    all_to_all x2, starting transfers between devices, kinship_apply(): lax.all_to_all(jnp.stack([field] * lax.axis_size('subj')), 'subj', 0, 0)  22.2 us
    all_to_all x1, blocking collectives, sent_to_all(): return lax.all_to_all(copies, axis, split_axis=0, concat_axis=0, tiled=True)  19.9 us
    another operation x4, local copies, waits for them, and re-layouts, kinship_apply(): slabs = gathered.reshape(-1, block, width)[kin_index[:, 1]]  16.5 us
    all_to_all x2, local copies, waits for them, and re-layouts, kinship_apply(): lax.all_to_all(jnp.stack([field] * lax.axis_size('subj')), 'subj', 0, 0)  8.11 us
  transfers between devices with their start and end apart: 2, of which 2 were waited for; matrix products, arithmetic and copies ran while one was open for 0% of the time, Pallas kernels for 0%

profile of v1, /device:TPU:1, one launch (start us, length us, event | category | flops | bytes accessed | tf_op | source)
XLA Modules:
  0.0 337.2 jit_solution(15145978828765659699)
XLA Ops:
  0.0 0.0 copy-start
  0.0 2.6 stack.4
  2.6 0.0 copy-start.2
  2.6 16.9 %all-to-all-start = ((bf16[32,2048,16]{1,2,0:T(8,128)(2,1)}), bf16[32,2048,16]{1,2,0:T(8,128)(2,1)}, u32[]{:S(2)}, u32[]{:S(2)}) async-start(bf16[32,2048,16]{1,2,0:T(8,128)(2,1)} %stack.4), calls=%async_computation | async-start | bytes 4194304 | tf_op jit(solution)/shard_map/all_to_all | solution.py:41
  19.5 0.0 copy-done.2
  19.5 98.6 %all-to-all-done = bf16[32,2048,16]{1,2,0:T(8,128)(2,1)} async-done(((bf16[32,2048,16]{1,2,0:T(8,128)(2,1)}), bf16[32,2048,16]{1,2,0:T(8,128)(2,1)}, u32[]{:S(2)}, u32[]{:S(2)}) %all-to-all-start) | async-done | bytes 2097184 | tf_op jit(solution)/shard_map/all_to_all | solution.py:41
  118.1 4.1 %copy.14 = bf16[32,2048,16]{1,0,2:T(8,128)(2,1)} copy(bf16[32,2048,16]{1,2,0:T(8,128)(2,1)} %all-to-all-done) | data formatting | bytes 4194304 | tf_op jit(solution)/shard_map/all_to_all | solution.py:41
  122.2 4.2 %reshape_reshape.6 = bf16[256,256,16]{1,0,2:T(8,128)(2,1)} reshape(bf16[32,2048,16]{1,0,2:T(8,128)(2,1)} %copy.14) | data formatting | bytes 4194304 | tf_op jit(solution)/shard_map/reshape;reshape | solution.py:43
  126.4 4.1 %copy.15 = bf16[256,256,16]{1,2,0:T(8,128)(2,1)} copy(bf16[256,256,16]{1,0,2:T(8,128)(2,1)} %reshape_reshape.6) | data formatting | bytes 4194304 | tf_op jit(solution)/shard_map/reshape;reshape | solution.py:43
  130.5 2.1 gather_fusion
  132.6 1.9 convolution_bitcast_fusion.2
  134.5 0.2 fusion.13
  134.7 1.6 stack.5
  136.3 5.2 %all-to-all-start.1 = ((bf16[32,2048,16]{1,2,0:T(8,128)(2,1)}), bf16[32,2048,16]{1,2,0:T(8,128)(2,1)}, u32[]{:S(2)}, u32[]{:S(2)}) async-start(bf16[32,2048,16]{1,2,0:T(8,128)(2,1)} %stack.5), calls=%async_computation.1 | async-start | bytes 4194304 | tf_op jit(solution)/shard_map/all_to_all | solution.py:41
  141.6 99.3 %all-to-all-done.1 = bf16[32,2048,16]{1,2,0:T(8,128)(2,1)} async-done(((bf16[32,2048,16]{1,2,0:T(8,128)(2,1)}), bf16[32,2048,16]{1,2,0:T(8,128)(2,1)}, u32[]{:S(2)}, u32[]{:S(2)}) %all-to-all-start.1) | async-done | bytes 2097184 | tf_op jit(solution)/shard_map/all_to_all | solution.py:41
  240.9 4.1 %copy.17 = bf16[32,2048,16]{1,0,2:T(8,128)(2,1)} copy(bf16[32,2048,16]{1,2,0:T(8,128)(2,1)} %all-to-all-done.1) | data formatting | bytes 4194304 | tf_op jit(solution)/shard_map/all_to_all | solution.py:41
  244.9 4.2 %reshape_reshape.7 = bf16[256,256,16]{1,0,2:T(8,128)(2,1)} reshape(bf16[32,2048,16]{1,0,2:T(8,128)(2,1)} %copy.17) | data formatting | bytes 4194304 | tf_op jit(solution)/shard_map/reshape;reshape | solution.py:43
  249.1 4.1 %copy.18 = bf16[256,256,16]{1,2,0:T(8,128)(2,1)} copy(bf16[256,256,16]{1,0,2:T(8,128)(2,1)} %reshape_reshape.7) | data formatting | bytes 4194304 | tf_op jit(solution)/shard_map/reshape;reshape | solution.py:43
  253.2 0.0 copy-start.1
  253.2 2.2 gather_fusion.1
  255.4 1.9 convolution_bitcast_fusion.1
  257.3 0.2 convolution_multiply_fusion
  257.5 0.0 copy-done.1
  257.6 0.1 broadcast_in_dim.2
  257.7 19.9 %all_to_all.20 = bf16[16,2048,16]{1,2,0:T(8,128)(2,1)S(1)} all-to-all(bf16[16,2048,16]{1,2,0:T(8,128)(2,1)S(1)} %broadcast_in_dim.2), channel_id=1, replica_groups=mesh['subj'=32,'var'=16] {'var'}, dimensions={0} | all-to-all | bytes 2097152 | tf_op jit(solution)/shard_map/all_to_all | solution.py:9
  277.6 0.0 copy-done
  277.6 1.9 convolution_bitcast_fusion
  279.4 2.3 copy.20
  281.7 53.6 %all_to_all.21 = f32[32,24,256]{2,1,0:T(8,128)} all-to-all(f32[32,24,256]{2,1,0:T(8,128)} %bitcast.42), channel_id=1, replica_groups=mesh['subj'=32,'var'=16] {'subj'}, dimensions={0} | all-to-all | bytes 1572864 | tf_op jit(solution)/shard_map/all_to_all | solution.py:31
  335.4 1.2 reduce_sum.9
  336.6 0.6 broadcast_multiply_fusion.1
  (6 shorter events, 0.2 us)
Async XLA Ops:
  0.0 277.6 %copy-start = (bf16[2048,768]{1,0:T(8,128)(2,1)S(1)}, bf16[2048,768]{1,0:T(8,128)(2,1)}, u32[]{:S(2)}) copy-start(bf16[2048,768]{1,0:T(8,128)(2,1)} %param.7) | copy-start | bytes 9437188
  2.6 17.0 %copy-start.2 = (s32[12,2]{0,1:T(2,128)S(1)}, s32[12,2]{0,1:T(2,128)}, u32[]{:S(2)}) copy-start(s32[12,2]{0,1:T(2,128)} %param.6) | copy-start | bytes 292
  2.6 115.6 %all-to-all-start = ((bf16[32,2048,16]{1,2,0:T(8,128)(2,1)}), bf16[32,2048,16]{1,2,0:T(8,128)(2,1)}, u32[]{:S(2)}, u32[]{:S(2)}) async-start(bf16[32,2048,16]{1,2,0:T(8,128)(2,1)} %stack.4), calls=%async_computation | async-start | bytes 4194304 | tf_op jit(solution)/shard_map/all_to_all | solution.py:41
  136.3 104.6 %all-to-all-start.1 = ((bf16[32,2048,16]{1,2,0:T(8,128)(2,1)}), bf16[32,2048,16]{1,2,0:T(8,128)(2,1)}, u32[]{:S(2)}, u32[]{:S(2)}) async-start(bf16[32,2048,16]{1,2,0:T(8,128)(2,1)} %stack.5), calls=%async_computation.1 | async-start | bytes 4194304 | tf_op jit(solution)/shard_map/all_to_all | solution.py:41
  253.2 4.3 %copy-start.1 = (bf16[2048,16]{0,1:T(8,128)(2,1)S(1)}, bf16[2048,16]{0,1:T(8,128)(2,1)}, u32[]{:S(2)}) copy-start(bf16[2048,16]{0,1:T(8,128)(2,1)} %param.4) | copy-start | bytes 196612
